TPU v7x, 32 devices: a whole 2x2x4 slice. The times are simulated.
32 devices in a mesh: narrow: 4 (over y, x), wide: 8 (over z, core).
Axes of the slice: x: 2, y: 2, z: 4, core: 2. Of those that a mesh axis runs over, the one named last changes fastest.
Arguments:
- slices: bfloat16 [32, 1024, 1024], P(None, 'narrow', 'wide'), may hold values from -6 to 6
- mode_one: bfloat16 [1024, 512], P('narrow', 'wide'), may hold values from -6 to 6
- mode_two: bfloat16 [1024, 512], P('wide', 'narrow'), may hold values from -6 to 6
- slice_table: bfloat16 [1024, 512], replicated, may hold values from 0.0099487305 to 0.079589844
- chosen: int32 [32], replicated, may hold values from 0 to 1023
Outputs:
- new_one: bfloat16 [1024, 512], P('narrow', 'wide')
- new_two: bfloat16 [1024, 512], P('wide', 'narrow')
All inputs are finite; a program needn't handle non-finite values.
Results may differ from a plain program's by a relative error of at most 0.006.
Values may be sent and summed in bfloat16 or wider, within the bound.
A program may use at most 64 MiB of HBM per device.

v0:
```python
import jax
import jax.numpy as jnp
from jax import lax
from jax.sharding import PartitionSpec as P

R = 512


epsilon = 1e-06
step_size = 0.5


def body(slices, mode_one, mode_two, slice_table, chosen):
    own_width = mode_one.shape[1]
    one_hot = (
        chosen[:, None]
        == lax.broadcasted_iota(jnp.int32, (chosen.shape[0], slice_table.shape[0]), 1)
    ).astype(jnp.bfloat16)
    slice_rows = jnp.dot(one_hot, slice_table, preferred_element_type=jnp.float32)
    target = slices.astype(jnp.float32)
    full_two = lax.all_gather(mode_two, "narrow", axis=1, tiled=True)
    full_one = lax.all_gather(mode_one, "wide", axis=1, tiled=True)
    scaled_two = (full_two.astype(jnp.float32)[None, :, :] * slice_rows[:, None, :]).astype(
        jnp.bfloat16
    )
    model_one = jnp.einsum("ir,kjr->kij", full_one, scaled_two, preferred_element_type=jnp.float32)
    error_one = jnp.tanh(model_one - target).astype(jnp.bfloat16)
    partial_one = jnp.einsum(
        "kij,kjr->ir", error_one, scaled_two, preferred_element_type=jnp.float32
    )
    grad_one = lax.psum(partial_one, "wide")
    inverse = lax.rsqrt(jnp.sum(grad_one * grad_one, axis=1, keepdims=True) / R + epsilon)
    new_full = (full_one.astype(jnp.float32) - step_size * grad_one * inverse).astype(jnp.bfloat16)
    offset = lax.axis_index("wide") * own_width
    new_one = lax.dynamic_slice_in_dim(new_full, offset, own_width, 1)
    scaled_one = (new_full.astype(jnp.float32)[None, :, :] * slice_rows[:, None, :]).astype(
        jnp.bfloat16
    )
    model_two = jnp.einsum("kir,jr->kij", scaled_one, full_two, preferred_element_type=jnp.float32)
    error_two = jnp.tanh(model_two - target).astype(jnp.bfloat16)
    partial_two = jnp.einsum(
        "kij,kir->jr", error_two, scaled_one, preferred_element_type=jnp.float32
    )
    grad_two = lax.psum_scatter(partial_two, "narrow", scatter_dimension=1, tiled=True)
    squares_two = lax.psum(jnp.sum(grad_two * grad_two, axis=1), "narrow")
    inverse_two = lax.rsqrt(squares_two / R + epsilon)
    new_two = (mode_two.astype(jnp.float32) - step_size * grad_two * inverse_two[:, None]).astype(
        jnp.bfloat16
    )
    return (new_one, new_two)


def solution(mesh):
    in_specs = (P(None, "narrow", "wide"), P("narrow", "wide"), P("wide", "narrow"), P(), P())
    out_specs = (P("narrow", "wide"), P("wide", "narrow"))
    return jax.shard_map(body, mesh=mesh, in_specs=in_specs, out_specs=out_specs, check_vma=False)
```

profile of v0, /device:TPU:0, one launch (start us, length us, event | category | flops | bytes accessed | tf_op | source)
XLA Modules:
  0.0 144.4 jit_solution(11126286288868886825)
XLA Ops:
  7.2 0.0 copy-start
  7.2 0.0 all-reduce.2.cloned.1.call-start
  7.2 10.2 %all_gather.7 = bf16[128,512]{1,0:T(8,128)(2,1)S(1)} all-gather(bf16[128,128]{1,0:T(8,128)(2,1)} %param.7), channel_id=1, replica_groups=mesh['narrow'=4,'wide'=8] {'narrow'}, dimensions={1}, use_global_device_ids=true | all-gather | bytes 163840 | tf_op jit(solution)/shard_map/all_gather | solution.py:21
  17.5 14.7 %all_gather.6 = bf16[256,512]{0,1:T(8,128)(2,1)S(1)} all-gather(bf16[256,64]{0,1:T(8,128)(2,1)} %param.6), channel_id=1, replica_groups=mesh['narrow'=4,'wide'=8] {'wide'}, dimensions={1}, use_global_device_ids=true | all-gather | bytes 294912 | tf_op jit(solution)/shard_map/all_gather | solution.py:22
  32.2 0.0 copy-done
  32.2 1.0 fusion.25
  33.1 5.0 %fusion.17 = f32[256,512]{1,0:T(8,128)} fusion(f32[32,512]{1,0:T(8,128)S(1)} %fusion.25, f32[128,512]{1,0:T(8,128)S(1)} %convert_element_type.35, bf16[32,256,128]{2,1,0:T(8,128)(2,1)} %param.5, bf16[256,512]{0,1:T(8,128)(2,1)S(1)} %all_gather.6), kind=kOutput, calls=%fused_computation.20 | convolution fusion | flops 2159017984 | bytes 3211264 | tf_op jit(solution)/shard_map/kij,kjr->ir/dot_general | solution.py:28
  38.1 0.0 all-reduce.2.cloned.1.call-update
  38.1 0.0 reduce-scatter.2.cloned.1.call-start
  38.2 0.1 copy.10
  38.3 56.2 %all-reduce.2.cloned.1.call-done = f32[256,512]{1,0:T(8,128)} async-done(((f32[256,512]{1,0:T(8,128)}), f32[256,512]{1,0:T(8,128)}) %all-reduce.2.cloned.1.call-update) | async-done | bytes 524304 | tf_op jit(solution)/shard_map/psum | solution.py:31
  94.5 1.2 multiply_reduce_fusion
  95.7 1.2 fusion.27
  96.9 0.0 copy-start.1
  96.9 5.9 %fusion.20 = f32[128,512]{1,0:T(8,128)} fusion(f32[32,512]{1,0:T(8,128)S(1)} %fusion.25, f32[256,512]{1,0:T(8,128)S(1)} %get-tuple-element.6, bf16[32,256,128]{2,1,0:T(8,128)(2,1)} %param.5, bf16[128,512]{1,0:T(8,128)(2,1)S(1)} %all_gather.7), kind=kOutput, calls=%fused_computation.21 | convolution fusion | flops 2167406592 | bytes 3080192 | tf_op jit(solution)/shard_map/kij,kir->jr/dot_general | solution.py:41
  102.8 0.0 reduce-scatter.2.cloned.1.call-update
  102.9 0.1 constant_dynamic-slice_fusion
  102.9 0.7 copy.12
  103.7 22.4 %reduce-scatter.2.cloned.1.call-done = f32[128,128]{1,0:T(8,128)} async-done(((f32[128,512]{1,0:T(8,128)}), f32[128,128]{1,0:T(8,128)}) %reduce-scatter.2.cloned.1.call-update) | async-done | bytes 65552 | tf_op jit(solution)/shard_map/reduce_scatter | solution.py:44
  126.1 0.9 multiply_reduce_fusion.1
  127.0 8.9 %psum.15 = f32[128]{0:T(128)S(1)} all-reduce(f32[128]{0:T(128)S(1)} %multiply_reduce_fusion.1), channel_id=1, replica_groups=mesh['narrow'=4,'wide'=8] {'narrow'}, use_global_device_ids=true, to_apply=%region_4.0 | all-reduce | flops 128 | bytes 1024 | tf_op jit(solution)/shard_map/psum | solution.py:45
  136.0 0.0 copy-done.1
  136.0 1.5 %subtract_convert_fusion.1 = bf16[128,128]{1,0:T(8,128)(2,1)} fusion(f32[128,128]{1,0:T(8,128)} %reduce-scatter.2.cloned.1.call-done, bf16[128,128]{1,0:T(8,128)(2,1)S(1)} %copy-done.1, f32[128]{0:T(128)S(1)} %rsqrt_multiply_fusion.1), kind=kLoop, calls=%fused_computation.28 | loop fusion | flops 65536 | bytes 131584 | tf_op jit(solution)/shard_map/convert_element_type | solution.py:47
  (3 shorter events, 0.0 us)
Async XLA Ops:
  7.2 25.0 %copy-start = (bf16[1024,512]{1,0:T(8,128)(2,1)S(1)}, bf16[1024,512]{1,0:T(8,128)(2,1)}, u32[]{:S(2)}) copy-start(bf16[1024,512]{1,0:T(8,128)(2,1)} %param.8) | copy-start | bytes 3145732
  7.2 87.3 %all-reduce.2.cloned.1.call-start = ((), (), s32[]{:S(2)}) async-start(), calls=%async_computation.1 | async-start | bytes 1048576 | tf_op jit(solution)/shard_map/psum | solution.py:31
  38.1 87.9 %reduce-scatter.2.cloned.1.call-start = ((), (), s32[]{:S(2)}) async-start(), calls=%async_computation.2 | async-start | bytes 327680 | tf_op jit(solution)/shard_map/reduce_scatter | solution.py:44
  96.9 39.1 %copy-start.1 = (bf16[128,128]{1,0:T(8,128)(2,1)S(1)}, bf16[128,128]{1,0:T(8,128)(2,1)}, u32[]{:S(2)}) copy-start(bf16[128,128]{1,0:T(8,128)(2,1)} %param.7) | copy-start | bytes 98308
Sparse Core Ops, SparseCore 0:
  38.2 56.2 all-reduce.1
  103.0 23.0 reduce-scatter.1
where the time goes:
time: 145 us; the launch traced here: 144 us
  waiting for transfers between devices  78.6 us (54%)
  blocking collectives  33.8 us (23%)
  between operations  14.1 us (10%)
  matrix products  11.9 us (8%)
  other arithmetic  4.85 us (3%)
    psum x1, waiting for transfers between devices, body(): grad_one = lax.psum(partial_one, 'wide')  56.2 us
    reduce_scatter x1, waiting for transfers between devices, body(): lax.psum_scatter(partial_two, 'narrow', scatter_dimension=1, tiled=True)  22.4 us
    all_gather x1, blocking collectives, body(): full_one = lax.all_gather(mode_one, 'wide', axis=1, tiled=True)  14.7 us
    all_gather x1, blocking collectives, body(): full_two = lax.all_gather(mode_two, 'narrow', axis=1, tiled=True)  10.2 us
    psum x1, blocking collectives, body(): squares_two = lax.psum(jnp.sum(grad_two * grad_two, axis=1), 'narrow')  8.95 us
    dot_general x1, matrix products, body(): jnp.einsum('kij,kir->jr', error_two, scaled_one, preferred_element_type=j...  5.94 us
    dot_general x1, matrix products, body(): jnp.einsum('kij,kjr->ir', error_one, scaled_two, preferred_element_type=j...  4.97 us
  transfers between devices with their start and end apart: 2, of which 2 were waited for; matrix products, arithmetic and copies ran while one was open for 1% of the time, Pallas kernels for 0%

commit v1 on v0

v1 whole, which is shorter than its diff:
```python
import functools
import jax
import jax.numpy as jnp
from jax import lax
from jax.experimental import pallas as pl
from jax.experimental.pallas import tpu as pltpu
from jax.sharding import PartitionSpec as P

epsilon = 1e-06
step_size = 0.5
f32 = jnp.float32
bf16 = jnp.bfloat16


def dot(a, b, dims):
    return lax.dot_general(a, b, (dims, ((), ())), preferred_element_type=f32)


def kernel(
    N, W, flip, step,
    slices_hbm, one_ref, two_ref, table_hbm, chosen_ref,
    out_one, out_two,
    slices, table, rows_s, one_t, two_blk, one_rows, two_rows, S, slices_t,
    grad, sib_in, rs_out, rs_in, new_rows, new_t, grad2, rs2_out, rs2_in, piece, piece_in,
    local_sem, gs, gr, fs, fr, ts, tr, ss, sr, rs, rr, ns, nr, ms, mr, us, ur, ps, pr,
):
    G = W // 2
    w = lax.axis_index("wide")
    n = lax.axis_index("narrow")
    g, c = w // 2, w % 2
    sib = {"wide": g * 2 + (1 - c)}
    K, I, J = slices.shape
    R = S.shape[1]

    def far(d):
        return {"wide": lax.rem(g + d, G) * 2 + c}

    def across(d):
        return {"narrow": lax.rem(n + d, N)}

    def send(src, dst, s, r, dev):
        copy = pltpu.make_async_remote_copy(
            src_ref=src, dst_ref=dst, send_sem=s, recv_sem=r,
            device_id=dev, device_id_type=pl.DeviceIdType.MESH,
        )
        copy.start()
        return copy

    load_table = pltpu.make_async_copy(table_hbm, table, local_sem.at[0])
    load_table.start()
    load_slices = pltpu.make_async_copy(slices_hbm, slices, local_sem.at[1])
    load_slices.start()

    barrier = pltpu.get_barrier_semaphore()
    partners = [sib] + [far(d) for d in range(1, G)] + [across(d) for d in range(1, N)]
    for dev in partners:
        pl.semaphore_signal(barrier, inc=1, device_id=dev, device_id_type=pl.DeviceIdType.MESH)
    pl.semaphore_wait(barrier, len(partners))

    sent = []

    def spread(own, buf, far_s, far_r, sib_s, sib_r):
        z = [send(own, buf.at[w], far_s.at[d], far_r.at[d], far(d)) for d in range(1, G)]
        f = [send(own, buf.at[w], sib_s.at[0], sib_r.at[0], sib)]

        def finish():
            for d in range(1, G):
                z[d - 1].wait_recv()
                at = buf.at[lax.rem(g - d + G, G) * 2 + c]
                f.append(send(at, at, sib_s.at[d], sib_r.at[d], sib))
            for copy in f:
                copy.wait_recv()
            sent.extend(z)
            sent.extend(f)

        return finish

    two_copies = [
        send(two_ref, two_blk.at[n], ts.at[d], tr.at[d], across(d)) for d in range(1, N)
    ]
    finish_one = spread(one_ref, one_t, gs, gr, fs, fr)
    two_blk[n] = two_ref[...]
    one_t[w] = one_ref[...]

    load_table.wait()
    hot = (
        lax.broadcasted_iota(jnp.int32, (table.shape[0], K), 0) == chosen_ref[...]
    ).astype(f32).astype(bf16)
    rows_s[...] = dot(hot, table[...], ((0,), (0,)))

    for copy in two_copies:
        copy.wait_recv()
    sent.extend(two_copies)
    if flip:
        two = two_blk[...].reshape(R, J).T
    else:
        two = jnp.concatenate([two_blk[m] for m in range(N)], axis=1)
    two_rows[...] = two.reshape(two_rows.shape)

    @pl.loop(0, K)
    def _(k):
        wide_two = two_rows[...].reshape(J, R).astype(f32)
        S[pl.ds(pl.multiple_of(k * J, J), J), :] = (wide_two * rows_s[pl.ds(k, 1), :]).astype(bf16)

    finish_one()
    one_rows[...] = one_t[...].reshape(R, I).T.reshape(one_rows.shape)
    load_slices.wait()
    grad[...] = jnp.zeros_like(grad)

    @pl.loop(0, K // step)
    def _(q):
        part = S[pl.ds(pl.multiple_of(q * step * J, step * J), step * J), :]
        model = dot(one_rows[...].reshape(I, R), part, ((1,), (1,)))
        target = jnp.concatenate([slices[q * step + m] for m in range(step)], axis=1)
        error = jnp.tanh(model - target.astype(f32)).astype(bf16)
        grad[...] += dot(error, part, ((1,), (0,))).reshape(grad.shape)

    halves = []
    for d in range(G):
        to = lax.rem(g + d + 1, G)
        halves.append(send(grad.at[to, 1 - c], sib_in.at[to], ss.at[d], sr.at[d], sib))
    shares = []
    for d in range(G):
        to = lax.rem(g + d + 1, G)
        halves[d].wait_recv()
        if d < G - 1:
            rs_out[to] = (grad[to, c] + sib_in[to]).astype(bf16)
            shares.append(send(rs_out.at[to], rs_in.at[g], rs.at[d], rr.at[d], far(d + 1)))
    total = grad[g, c] + sib_in[g]
    sent.extend(halves)

    @pl.loop(0, K)
    def _(k):
        slices_t[pl.ds(pl.multiple_of(k * J, J), J), :] = slices[k].T

    for d in range(G - 1):
        shares[d].wait_recv()
        total = total + rs_in[lax.rem(g - d - 1 + G, G)].astype(f32)
    sent.extend(shares)
    inverse = lax.rsqrt(jnp.sum(total * total, axis=1, keepdims=True) / R + epsilon)
    new_rows[w] = (one_rows[w].astype(f32) - step_size * total * inverse).astype(bf16)
    finish_new = spread(new_rows.at[w], new_rows, ns, nr, ms, mr)
    finish_new()
    new_t[...] = new_rows[...].reshape(I, R).T.reshape(new_t.shape)
    grad2[...] = jnp.zeros_like(grad2)

    @pl.loop(0, K // step)
    def _(q):
        at = pl.ds(pl.multiple_of(q * step * J, step * J), step * J)
        model = dot(S[at, :], new_t[...].reshape(R, I), ((1,), (0,)))
        error = jnp.tanh(model - slices_t[at, :].astype(f32)).astype(bf16)
        back = dot(error, new_rows[...].reshape(I, R), ((1,), (0,)))
        part = back[:J] * rows_s[pl.ds(q * step, 1), :]
        for m in range(1, step):
            part = part + back[m * J : (m + 1) * J] * rows_s[pl.ds(q * step + m, 1), :]
        grad2[...] += part.reshape(grad2.shape)

    rs2_out[...] = grad2[...].astype(bf16)
    shares2 = [
        send(rs2_out.at[lax.rem(n + d, N)], rs2_in.at[n], us.at[d], ur.at[d], across(d))
        for d in range(1, N)
    ]
    out_one[...] = new_t[w]
    total2 = grad2[n]
    for d in range(1, N):
        shares2[d - 1].wait_recv()
        total2 = total2 + rs2_in[lax.rem(n - d + N, N)].astype(f32)
    sent.extend(shares2)
    inverse2 = lax.rsqrt(jnp.sum(total2 * total2, axis=1, keepdims=True) / R + epsilon)
    fresh = (two_rows[n].astype(f32) - step_size * total2 * inverse2).astype(bf16)
    cols = R // N
    for m in range(N):
        piece[m] = fresh[:, m * cols : (m + 1) * cols]
    pieces = [
        send(piece.at[lax.rem(n + d, N)], piece_in.at[n], ps.at[d], pr.at[d], across(d))
        for d in range(1, N)
    ]
    piece_in[n] = piece[n]
    for copy in pieces:
        copy.wait_recv()
    out_two[...] = piece_in[...]
    sent.extend(pieces)
    for copy in sent:
        copy.wait_send()


def solution(mesh):
    N, W = mesh.shape["narrow"], mesh.shape["wide"]
    G = W // 2

    def body(slices, mode_one, mode_two, slice_table, chosen):
        K, I, J = slices.shape
        c1, c2 = mode_one.shape[1], mode_two.shape[1]
        R = c1 * W
        flip = c2 % 128 != 0
        step = next(s for s in (4, 2, 1) if K % s == 0)
        io, jo = I // W, J // N
        vm = pltpu.VMEM
        dma = pltpu.SemaphoreType.DMA
        in_vmem = pl.BlockSpec(memory_space=pltpu.VMEM)
        in_any = pl.BlockSpec(memory_space=pl.ANY)
        two = mode_two.T if flip else mode_two
        flops = 8 * K * I * J * R
        new_one, new_two = pl.pallas_call(
            functools.partial(kernel, N, W, flip, step),
            out_shape=(
                jax.ShapeDtypeStruct((c1, I), bf16),
                jax.ShapeDtypeStruct((N, jo, c2), bf16),
            ),
            in_specs=[in_any, in_vmem, in_vmem, in_any, in_vmem],
            out_specs=(in_vmem, in_vmem),
            scratch_shapes=[
                vm((K, I, J), bf16),
                vm(slice_table.shape, bf16),
                vm((K, R), f32),
                vm((W, c1, I), bf16),
                vm((N,) + two.shape, bf16),
                vm((W, io, R), bf16),
                vm((N, jo, R), bf16),
                vm((K * J, R), bf16),
                vm((K * J, I), bf16),
                vm((G, 2, io, R), f32),
                vm((G, io, R), f32),
                vm((G, io, R), bf16),
                vm((G, io, R), bf16),
                vm((W, io, R), bf16),
                vm((W, c1, I), bf16),
                vm((N, jo, R), f32),
                vm((N, jo, R), bf16),
                vm((N, jo, R), bf16),
                vm((N, jo, c2), bf16),
                vm((N, jo, c2), bf16),
                dma((2,)),
                dma((G,)), dma((G,)), dma((G,)), dma((G,)),
                dma((N,)), dma((N,)),
                dma((G,)), dma((G,)), dma((G,)), dma((G,)),
                dma((G,)), dma((G,)), dma((G,)), dma((G,)),
                dma((N,)), dma((N,)), dma((N,)), dma((N,)),
            ],
            compiler_params=pltpu.CompilerParams(
                collective_id=0, has_side_effects=True, vmem_limit_bytes=48 * 1024 * 1024
            ),
            cost_estimate=pl.CostEstimate(
                flops=flops, bytes_accessed=K * I * J * 2, transcendentals=2 * K * I * J
            ),
        )(slices, mode_one.T, two, slice_table, chosen.reshape(1, K))
        return new_one.T, new_two.reshape(J, c2)

    in_specs = (P(None, "narrow", "wide"), P("narrow", "wide"), P("wide", "narrow"), P(), P())
    out_specs = (P("narrow", "wide"), P("wide", "narrow"))
    return jax.shard_map(body, mesh=mesh, in_specs=in_specs, out_specs=out_specs, check_vma=False)
```

time: 145 us -> 46.2 us (0.32)
  waiting for transfers between devices: 78.6 us -> 0 us
  Pallas kernels: 0 us -> 39 us
  blocking collectives: 33.8 us -> 0 us
  between operations: 14.1 us -> 0.65 us
  matrix products: 11.9 us -> 0 us
  local copies, waits for them, and re-layouts: 0.96 us -> 6.21 us
  other arithmetic: 4.85 us -> 0 us
    psum x1 -> x0, waiting for transfers between devices: 56.2 us -> none  [body(): grad_one = lax.psum(partial_one, 'wide')]
    pallas_call x0 -> x1, Pallas kernels: none -> 39 us  [body(): pl.pallas_call(functools.partial(kernel, N, W, flip, step), out_shape=(ja...]
    all_gather x2 -> x0, blocking collectives: 24.9 us -> none  [the longest x1 14.7 us: body(): full_one = lax.all_gather(mode_one, 'wide', axis=1, tiled=True)]
    reduce_scatter x1 -> x0, waiting for transfers between devices: 22.4 us -> none  [body(): lax.psum_scatter(partial_two, 'narrow', scatter_dimension=1, tiled=True)]
    dot_general x3 -> x0, matrix products: 11.9 us -> none  [the longest x1 5.94 us: body(): jnp.einsum('kij,kir->jr', error_two, scaled_one, preferred_element_type=j...]
    psum x1 -> x0, blocking collectives: 8.95 us -> none  [body(): squares_two = lax.psum(jnp.sum(grad_two * grad_two, axis=1), 'narrow')]
    unnamed x5 -> x12, local copies, waits for them, and re-layouts: 0.73 us -> 6.21 us
    convert_element_type x3 -> x0, other arithmetic: 2.74 us -> none  [the longest x1 1.55 us: body(): (mode_two.astype(jnp.float32) - step_size * grad_two * inverse_two[:, Non...]
  transfers between devices with their start and end apart: 2 -> 0, of which waited for: 2 -> 0; matrix products, arithmetic and copies ran while one was open for 1% -> 0% of each run, Pallas kernels for 0% -> 0%
where the time goes in v1:
time: 46.2 us; the launch traced here: 45.8 us
  Pallas kernels  39 us (84%)
  local copies, waits for them, and re-layouts  6.21 us (13%)
  between operations  0.65 us (1%)
    pallas_call x1, Pallas kernels, body(): pl.pallas_call(functools.partial(kernel, N, W, flip, step), out_shape=(ja...  39 us
    unnamed x12, local copies, waits for them, and re-layouts  6.21 us

profile of v1, /device:TPU:0, one launch (start us, length us, event | category | flops | bytes accessed | tf_op | source)
XLA Modules:
  0.0 45.8 jit_solution(16613912835450675776)
XLA Ops:
  0.6 0.0 copy-start
  0.6 1.6 %copy-done = bf16[32,256,128]{2,1,0:T(8,128)(2,1)S(1)} copy-done((bf16[32,256,128]{2,1,0:T(8,128)(2,1)S(1)}, bf16[32,256,128]{2,1,0:T(8,128)(2,1)}, u32[]{:S(2)}) %copy-start) | copy-done | bytes 2097176
  2.2 0.0 copy-start.1
  2.2 1.2 %copy-done.1 = bf16[1024,512]{1,0:T(8,128)(2,1)S(1)} copy-done((bf16[1024,512]{1,0:T(8,128)(2,1)S(1)}, bf16[1024,512]{1,0:T(8,128)(2,1)}, u32[]{:S(2)}) %copy-start.1) | copy-done | bytes 1048600
  3.4 0.0 copy-start.2
  3.5 0.8 %copy-done.2 = bf16[256,64]{0,1:T(8,128)(2,1)S(1)} copy-done((bf16[256,64]{0,1:T(8,128)(2,1)S(1)}, bf16[256,64]{0,1:T(8,128)(2,1)}, u32[]{:S(2)}) %copy-start.2) | copy-done | bytes 32792
  4.2 0.0 copy-start.3
  4.2 0.8 %copy-done.3 = bf16[128,128]{1,0:T(8,128)(2,1)S(1)} copy-done((bf16[128,128]{1,0:T(8,128)(2,1)S(1)}, bf16[128,128]{1,0:T(8,128)(2,1)}, u32[]{:S(2)}) %copy-start.3) | copy-done | bytes 32792
  5.0 0.0 copy-start.4
  5.0 0.7 %copy-done.4 = s32[32]{0:T(128)S(1)} copy-done((s32[32]{0:T(128)S(1)}, s32[32]{0:T(128)}, u32[]{:S(2)}) %copy-start.4) | copy-done | bytes 152
  5.6 39.0 %shard_map.68 = (bf16[64,256]{1,0:T(8,128)(2,1)S(1)}, bf16[4,32,128]{2,1,0:T(8,128)(2,1)S(1)}) custom-call(bf16[32,256,128]{2,1,0:T(8,128)(2,1)S(1)} %copy-done, bf16[64,256]{1,0:T(8,128)(2,1)S(1)} %bitcast.6, bf16[128,128]{1,0:T(8,128)(2,1)S(1)} %copy-done.3, bf16[1024,512]{1,0:T(8,128)(2,1)S(1)} %copy-done.1, s32[1,32]{1,0:T(1,128)S(1)} %bitcast.7), custom_call_target="tpu_custom_call" | custom-call | flops 4294967296 | bytes 2097152 | tf_op jit(solution)/shard_map/pallas_call | solution.py:204
  44.6 0.6 %copy.9 = bf16[256,64]{0,1:T(8,128)(2,1)} copy(bf16[256,64]{0,1:T(8,128)(2,1)S(1)} %bitcast.5) | data formatting | bytes 65536
  45.2 0.6 %copy.10 = bf16[128,128]{1,0:T(8,128)(2,1)} copy(bf16[128,128]{1,0:T(8,128)(2,1)S(1)} %bitcast.4) | data formatting | bytes 65536
Async XLA Ops:
  0.6 1.6 %copy-start = (bf16[32,256,128]{2,1,0:T(8,128)(2,1)S(1)}, bf16[32,256,128]{2,1,0:T(8,128)(2,1)}, u32[]{:S(2)}) copy-start(bf16[32,256,128]{2,1,0:T(8,128)(2,1)} %slices_hbm.1) | copy-start | bytes 6291460
  2.2 1.2 %copy-start.1 = (bf16[1024,512]{1,0:T(8,128)(2,1)S(1)}, bf16[1024,512]{1,0:T(8,128)(2,1)}, u32[]{:S(2)}) copy-start(bf16[1024,512]{1,0:T(8,128)(2,1)} %table_hbm.1) | copy-start | bytes 3145732
  3.4 0.8 %copy-start.2 = (bf16[256,64]{0,1:T(8,128)(2,1)S(1)}, bf16[256,64]{0,1:T(8,128)(2,1)}, u32[]{:S(2)}) copy-start(bf16[256,64]{0,1:T(8,128)(2,1)} %param.6) | copy-start | bytes 98308
  4.2 0.8 %copy-start.3 = (bf16[128,128]{1,0:T(8,128)(2,1)S(1)}, bf16[128,128]{1,0:T(8,128)(2,1)}, u32[]{:S(2)}) copy-start(bf16[128,128]{1,0:T(8,128)(2,1)} %two_ref.1) | copy-start | bytes 98308
  5.0 0.7 %copy-start.4 = (s32[32]{0:T(128)S(1)}, s32[32]{0:T(128)}, u32[]{:S(2)}) copy-start(s32[32]{0:T(128)} %param.9) | copy-start | bytes 388

commit v2 on v1

--- a/solution.py
+++ b/solution.py
@@ -18,9 +18,9 @@
 
 def kernel(
     N, W, flip, step,
-    slices_hbm, one_ref, two_ref, table_hbm, chosen_ref,
-    out_one, out_two,
-    slices, table, rows_s, one_t, two_blk, one_rows, two_rows, S, slices_t,
+    slices_hbm, one_hbm, two_hbm, table_hbm, chosen_hbm,
+    one_out, two_out,
+    slices, table, chosen, rows_s, one_t, two_blk, one_rows, two_rows, S, slices_t,
     grad, sib_in, rs_out, rs_in, new_rows, new_t, grad2, rs2_out, rs2_in, piece, piece_in,
     local_sem, gs, gr, fs, fr, ts, tr, ss, sr, rs, rr, ns, nr, ms, mr, us, ur, ps, pr,
 ):
@@ -48,6 +48,12 @@
 
     load_table = pltpu.make_async_copy(table_hbm, table, local_sem.at[0])
     load_table.start()
+    load_chosen = pltpu.make_async_copy(chosen_hbm, chosen, local_sem.at[2])
+    load_chosen.start()
+    load_two = pltpu.make_async_copy(two_hbm, two_blk.at[n], local_sem.at[3])
+    load_two.start()
+    load_one = pltpu.make_async_copy(one_hbm, one_t.at[w], local_sem.at[4])
+    load_one.start()
     load_slices = pltpu.make_async_copy(slices_hbm, slices, local_sem.at[1])
     load_slices.start()
 
@@ -55,9 +61,25 @@
     partners = [sib] + [far(d) for d in range(1, G)] + [across(d) for d in range(1, N)]
     for dev in partners:
         pl.semaphore_signal(barrier, inc=1, device_id=dev, device_id_type=pl.DeviceIdType.MESH)
+    load_table.wait()
+    load_chosen.wait()
+    hot = (
+        lax.broadcasted_iota(jnp.int32, (table.shape[0], K), 0) == chosen[...]
+    ).astype(f32).astype(bf16)
+    rows_s[...] = dot(hot, table[...], ((0,), (0,)))
+    load_slices.wait()
+
+    @pl.loop(0, K)
+    def _(k):
+        slices_t[pl.ds(pl.multiple_of(k * J, J), J), :] = slices[k].T
+
     pl.semaphore_wait(barrier, len(partners))
 
     sent = []
+
+    def sweep():
+        while sent:
+            sent.pop().wait_send()
 
     def spread(own, buf, far_s, far_r, sib_s, sib_r):
         z = [send(own, buf.at[w], far_s.at[d], far_r.at[d], far(d)) for d in range(1, G)]
@@ -76,18 +98,11 @@
         return finish
 
     two_copies = [
-        send(two_ref, two_blk.at[n], ts.at[d], tr.at[d], across(d)) for d in range(1, N)
+        send(two_hbm, two_blk.at[n], ts.at[d], tr.at[d], across(d)) for d in range(1, N)
     ]
-    finish_one = spread(one_ref, one_t, gs, gr, fs, fr)
-    two_blk[n] = two_ref[...]
-    one_t[w] = one_ref[...]
-
-    load_table.wait()
-    hot = (
-        lax.broadcasted_iota(jnp.int32, (table.shape[0], K), 0) == chosen_ref[...]
-    ).astype(f32).astype(bf16)
-    rows_s[...] = dot(hot, table[...], ((0,), (0,)))
-
+    finish_one = spread(one_hbm, one_t, gs, gr, fs, fr)
+
+    load_two.wait()
     for copy in two_copies:
         copy.wait_recv()
     sent.extend(two_copies)
@@ -102,12 +117,12 @@
         wide_two = two_rows[...].reshape(J, R).astype(f32)
         S[pl.ds(pl.multiple_of(k * J, J), J), :] = (wide_two * rows_s[pl.ds(k, 1), :]).astype(bf16)
 
+    load_one.wait()
     finish_one()
     one_rows[...] = one_t[...].reshape(R, I).T.reshape(one_rows.shape)
-    load_slices.wait()
     grad[...] = jnp.zeros_like(grad)
 
-    @pl.loop(0, K // step)
+    @pl.loop(0, K // step, unroll=4)
     def _(q):
         part = S[pl.ds(pl.multiple_of(q * step * J, step * J), step * J), :]
         model = dot(one_rows[...].reshape(I, R), part, ((1,), (1,)))
@@ -115,6 +130,7 @@
         error = jnp.tanh(model - target.astype(f32)).astype(bf16)
         grad[...] += dot(error, part, ((1,), (0,))).reshape(grad.shape)
 
+    sweep()
     halves = []
     for d in range(G):
         to = lax.rem(g + d + 1, G)
@@ -129,10 +145,7 @@
     total = grad[g, c] + sib_in[g]
     sent.extend(halves)
 
-    @pl.loop(0, K)
-    def _(k):
-        slices_t[pl.ds(pl.multiple_of(k * J, J), J), :] = slices[k].T
-
+    sweep()
     for d in range(G - 1):
         shares[d].wait_recv()
         total = total + rs_in[lax.rem(g - d - 1 + G, G)].astype(f32)
@@ -144,7 +157,7 @@
     new_t[...] = new_rows[...].reshape(I, R).T.reshape(new_t.shape)
     grad2[...] = jnp.zeros_like(grad2)
 
-    @pl.loop(0, K // step)
+    @pl.loop(0, K // step, unroll=4)
     def _(q):
         at = pl.ds(pl.multiple_of(q * step * J, step * J), step * J)
         model = dot(S[at, :], new_t[...].reshape(R, I), ((1,), (0,)))
@@ -160,7 +173,8 @@
         send(rs2_out.at[lax.rem(n + d, N)], rs2_in.at[n], us.at[d], ur.at[d], across(d))
         for d in range(1, N)
     ]
-    out_one[...] = new_t[w]
+    one_out[...] = new_t[w]
+    sweep()
     total2 = grad2[n]
     for d in range(1, N):
         shares2[d - 1].wait_recv()
@@ -176,12 +190,12 @@
         for d in range(1, N)
     ]
     piece_in[n] = piece[n]
+    sweep()
     for copy in pieces:
         copy.wait_recv()
-    out_two[...] = piece_in[...]
+    two_out[...] = piece_in[...]
     sent.extend(pieces)
-    for copy in sent:
-        copy.wait_send()
+    sweep()
 
 
 def solution(mesh):
@@ -193,12 +207,11 @@
         c1, c2 = mode_one.shape[1], mode_two.shape[1]
         R = c1 * W
         flip = c2 % 128 != 0
-        step = next(s for s in (4, 2, 1) if K % s == 0)
+        step = next(s for s in (8, 4, 2, 1) if K % s == 0)
         io, jo = I // W, J // N
         vm = pltpu.VMEM
         dma = pltpu.SemaphoreType.DMA
-        in_vmem = pl.BlockSpec(memory_space=pltpu.VMEM)
-        in_any = pl.BlockSpec(memory_space=pl.ANY)
+        in_hbm = pl.BlockSpec(memory_space=pltpu.HBM)
         two = mode_two.T if flip else mode_two
         flops = 8 * K * I * J * R
         new_one, new_two = pl.pallas_call(
@@ -207,11 +220,12 @@
                 jax.ShapeDtypeStruct((c1, I), bf16),
                 jax.ShapeDtypeStruct((N, jo, c2), bf16),
             ),
-            in_specs=[in_any, in_vmem, in_vmem, in_any, in_vmem],
-            out_specs=(in_vmem, in_vmem),
+            in_specs=[in_hbm] * 5,
+            out_specs=(pl.BlockSpec(memory_space=pltpu.VMEM),) * 2,
             scratch_shapes=[
                 vm((K, I, J), bf16),
                 vm(slice_table.shape, bf16),
+                vm((1, K), jnp.int32),
                 vm((K, R), f32),
                 vm((W, c1, I), bf16),
                 vm((N,) + two.shape, bf16),
@@ -230,7 +244,7 @@
                 vm((N, jo, R), bf16),
                 vm((N, jo, c2), bf16),
                 vm((N, jo, c2), bf16),
-                dma((2,)),
+                dma((5,)),
                 dma((G,)), dma((G,)), dma((G,)), dma((G,)),
                 dma((N,)), dma((N,)),
                 dma((G,)), dma((G,)), dma((G,)), dma((G,)),
@@ -238,7 +252,7 @@
                 dma((N,)), dma((N,)), dma((N,)), dma((N,)),
             ],
             compiler_params=pltpu.CompilerParams(
-                collective_id=0, has_side_effects=True, vmem_limit_bytes=48 * 1024 * 1024
+                collective_id=0, has_side_effects=True, vmem_limit_bytes=60 * 1024 * 1024
             ),
             cost_estimate=pl.CostEstimate(
                 flops=flops, bytes_accessed=K * I * J * 2, transcendentals=2 * K * I * J

time: 46.2 us -> 39.8 us (0.86)
  local copies, waits for them, and re-layouts: 6.21 us -> 2.75 us
  Pallas kernels: 39 us -> 36.2 us
    unnamed x12 -> x2, local copies, waits for them, and re-layouts: 6.21 us -> 2.75 us
    pallas_call x1, Pallas kernels: 39 us -> 36.2 us  [body(): pl.pallas_call(functools.partial(kernel, N, W, flip, step), out_shape=(ja...]
where the time goes in v2:
time: 39.8 us; the launch traced here: 39.6 us
  Pallas kernels  36.2 us (91%)
  local copies, waits for them, and re-layouts  2.75 us (7%)
  between operations  0.64 us (2%)
    pallas_call x1, Pallas kernels, body(): pl.pallas_call(functools.partial(kernel, N, W, flip, step), out_shape=(ja...  36.2 us
    unnamed x2, local copies, waits for them, and re-layouts  2.75 us

profile of v2, /device:TPU:0, one launch (start us, length us, event | category | flops | bytes accessed | tf_op | source)
XLA Modules:
  0.0 39.6 jit_solution(9701776291259837233)
XLA Ops:
  0.6 36.2 %shard_map.68 = (bf16[64,256]{1,0:T(8,128)(2,1)}, bf16[4,32,128]{2,1,0:T(8,128)(2,1)}) custom-call(bf16[32,256,128]{2,1,0:T(8,128)(2,1)} %slices_hbm.1, bf16[64,256]{1,0:T(8,128)(2,1)} %bitcast.6, bf16[128,128]{1,0:T(8,128)(2,1)} %two_hbm.1, bf16[1024,512]{1,0:T(8,128)(2,1)} %table_hbm.1, s32[1,32]{1,0:T(1,128)} %bitcast.7), custom_call_target="tpu_custom_call" | custom-call | flops 4294967296 | bytes 2097152 | tf_op jit(solution)/shard_map/pallas_call | solution.py:217
  36.8 1.4 %copy.9 = bf16[256,64]{0,1:T(8,128)(2,1)} copy(bf16[256,64]{0,1:T(8,128)(2,1)} %bitcast.5) | data formatting | bytes 65536
  38.2 1.4 %copy.10 = bf16[128,128]{1,0:T(8,128)(2,1)} copy(bf16[128,128]{1,0:T(8,128)(2,1)} %bitcast.4) | data formatting | bytes 65536

commit v3 on v2

--- a/solution.py
+++ b/solution.py
@@ -69,7 +69,7 @@
     rows_s[...] = dot(hot, table[...], ((0,), (0,)))
     load_slices.wait()
 
-    @pl.loop(0, K)
+    @pl.loop(0, K, unroll=4)
     def _(k):
         slices_t[pl.ds(pl.multiple_of(k * J, J), J), :] = slices[k].T
 
@@ -112,7 +112,7 @@
         two = jnp.concatenate([two_blk[m] for m in range(N)], axis=1)
     two_rows[...] = two.reshape(two_rows.shape)
 
-    @pl.loop(0, K)
+    @pl.loop(0, K, unroll=4)
     def _(k):
         wide_two = two_rows[...].reshape(J, R).astype(f32)
         S[pl.ds(pl.multiple_of(k * J, J), J), :] = (wide_two * rows_s[pl.ds(k, 1), :]).astype(bf16)
@@ -196,6 +196,15 @@
     two_out[...] = piece_in[...]
     sent.extend(pieces)
     sweep()
+
+
+def settle(one_ref, two_ref, one_out, two_out, sem):
+    first = pltpu.make_async_copy(one_ref, one_out, sem.at[0])
+    second = pltpu.make_async_copy(two_ref, two_out, sem.at[1])
+    first.start()
+    second.start()
+    first.wait()
+    second.wait()
 
 
 def solution(mesh):
@@ -258,6 +267,18 @@
                 flops=flops, bytes_accessed=K * I * J * 2, transcendentals=2 * K * I * J
             ),
         )(slices, mode_one.T, two, slice_table, chosen.reshape(1, K))
+        vspec = pl.BlockSpec(memory_space=pltpu.VMEM)
+        new_one, new_two = pl.pallas_call(
+            settle,
+            out_shape=(
+                jax.ShapeDtypeStruct(new_one.shape, bf16),
+                jax.ShapeDtypeStruct(new_two.shape, bf16),
+            ),
+            in_specs=[vspec] * 2,
+            out_specs=(pl.BlockSpec(memory_space=pl.ANY),) * 2,
+            scratch_shapes=[pltpu.SemaphoreType.DMA((2,))],
+            compiler_params=pltpu.CompilerParams(vmem_limit_bytes=60 * 1024 * 1024),
+        )(new_one, new_two)
         return new_one.T, new_two.reshape(J, c2)
 
     in_specs = (P(None, "narrow", "wide"), P("narrow", "wide"), P("wide", "narrow"), P(), P())

time: 39.8 us -> 37 us (0.930)
  local copies, waits for them, and re-layouts: 2.75 us -> 0 us
    unnamed x2 -> x0, local copies, waits for them, and re-layouts: 2.75 us -> none
    pallas_call x1, Pallas kernels: 36.2 us -> 34.7 us  [body(): pl.pallas_call(functools.partial(kernel, N, W, flip, step), out_shape=(ja...]
    pallas_call x0 -> x1, Pallas kernels: none -> 1.42 us  [body(): pl.pallas_call(settle, out_shape=(jax.ShapeDtypeStruct(new_one.shape, bf1...]
where the time goes in v3:
time: 37 us; the launch traced here: 36.8 us
  Pallas kernels  36.2 us (98%)
  between operations  0.64 us (2%)
    pallas_call x1, Pallas kernels, body(): pl.pallas_call(functools.partial(kernel, N, W, flip, step), out_shape=(ja...  34.7 us
    pallas_call x1, Pallas kernels, body(): pl.pallas_call(settle, out_shape=(jax.ShapeDtypeStruct(new_one.shape, bf1...  1.42 us

profile of v3, /device:TPU:0, one launch (start us, length us, event | category | flops | bytes accessed | tf_op | source)
XLA Modules:
  0.0 36.8 jit_solution(7483044964507488467)
XLA Ops:
  0.6 34.7 %shard_map.68 = (bf16[64,256]{1,0:T(8,128)(2,1)}, bf16[4,32,128]{2,1,0:T(8,128)(2,1)}) custom-call(bf16[32,256,128]{2,1,0:T(8,128)(2,1)} %slices_hbm.1, bf16[64,256]{1,0:T(8,128)(2,1)} %bitcast.4, bf16[128,128]{1,0:T(8,128)(2,1)} %two_hbm.1, bf16[1024,512]{1,0:T(8,128)(2,1)} %table_hbm.1, s32[1,32]{1,0:T(1,128)} %bitcast.7), custom_call_target="tpu_custom_call" | custom-call | flops 4294967296 | bytes 2097152 | tf_op jit(solution)/shard_map/pallas_call | solution.py:226
  35.4 1.4 %shard_map.69 = (bf16[64,256]{1,0:T(8,128)(2,1)}, bf16[4,32,128]{2,1,0:T(8,128)(2,1)}) custom-call(bf16[64,256]{1,0:T(8,128)(2,1)} %get-tuple-element.6.one_ref, bf16[4,32,128]{2,1,0:T(8,128)(2,1)} %get-tuple-element.7.two_ref), custom_call_target="tpu_custom_call" | custom-call | tf_op jit(solution)/shard_map/pallas_call | solution.py:271

commit v4 on v3

--- a/solution.py
+++ b/solution.py
@@ -69,7 +69,7 @@
     rows_s[...] = dot(hot, table[...], ((0,), (0,)))
     load_slices.wait()
 
-    @pl.loop(0, K, unroll=4)
+    @pl.loop(0, K, unroll=8)
     def _(k):
         slices_t[pl.ds(pl.multiple_of(k * J, J), J), :] = slices[k].T
 
@@ -112,7 +112,7 @@
         two = jnp.concatenate([two_blk[m] for m in range(N)], axis=1)
     two_rows[...] = two.reshape(two_rows.shape)
 
-    @pl.loop(0, K, unroll=4)
+    @pl.loop(0, K, unroll=8)
     def _(k):
         wide_two = two_rows[...].reshape(J, R).astype(f32)
         S[pl.ds(pl.multiple_of(k * J, J), J), :] = (wide_two * rows_s[pl.ds(k, 1), :]).astype(bf16)

time: 37 us -> 37.1 us (level)
  no operation moved by 1% of the time
where the time goes in v4:
time: 37.1 us; the launch traced here: 36.9 us
  Pallas kernels  36.3 us (98%)
  between operations  0.64 us (2%)
    pallas_call x1, Pallas kernels, body(): pl.pallas_call(functools.partial(kernel, N, W, flip, step), out_shape=(ja...  34.9 us
    pallas_call x1, Pallas kernels, body(): pl.pallas_call(settle, out_shape=(jax.ShapeDtypeStruct(new_one.shape, bf1...  1.42 us

profile of v4, /device:TPU:0, one launch (start us, length us, event | category | flops | bytes accessed | tf_op | source)
XLA Modules:
  0.0 36.9 jit_solution(12044337776658548587)
XLA Ops:
  0.6 34.9 %shard_map.68 = (bf16[64,256]{1,0:T(8,128)(2,1)}, bf16[4,32,128]{2,1,0:T(8,128)(2,1)}) custom-call(bf16[32,256,128]{2,1,0:T(8,128)(2,1)} %slices_hbm.1, bf16[64,256]{1,0:T(8,128)(2,1)} %bitcast.4, bf16[128,128]{1,0:T(8,128)(2,1)} %two_hbm.1, bf16[1024,512]{1,0:T(8,128)(2,1)} %table_hbm.1, s32[1,32]{1,0:T(1,128)} %bitcast.7), custom_call_target="tpu_custom_call" | custom-call | flops 4294967296 | bytes 2097152 | tf_op jit(solution)/shard_map/pallas_call | solution.py:226
  35.5 1.4 %shard_map.69 = (bf16[64,256]{1,0:T(8,128)(2,1)}, bf16[4,32,128]{2,1,0:T(8,128)(2,1)}) custom-call(bf16[64,256]{1,0:T(8,128)(2,1)} %get-tuple-element.6.one_ref, bf16[4,32,128]{2,1,0:T(8,128)(2,1)} %get-tuple-element.7.two_ref), custom_call_target="tpu_custom_call" | custom-call | tf_op jit(solution)/shard_map/pallas_call | solution.py:271
